TPU v7x, 1024 devices: a whole 8x8x8 slice. The times are simulated.
1024 devices in a mesh: dp: 32 (over y, z_hi), tower: 32 (over z_lo, x, core).
Axes of the slice: x: 8, y: 8, z: 8 (z_hi: 4, z_lo: 2; z = z_hi * 2 + z_lo), core: 2. Of those that a mesh axis runs over, the one named last changes fastest.
Arguments:
- learner_image: bfloat16 [16384, 1152], P('dp')
- learner_text: bfloat16 [16384, 1152], P('dp')
- ref_image: bfloat16 [16384, 1152], P('dp')
- ref_text: bfloat16 [16384, 1152], P('dp')
- head_weight: bfloat16 [1152, 1152], P('tower'), may hold values from -0.1875 to 0.1875
- kept_index: int32 [8192], P('dp'), may hold values from 0 to 511, as said below
- kept_owner: int32 [8192, 1], P('dp'), may hold values from 0 to 31; in each aligned block of 256 rows (0 to 255, 256 to 511, ...) at most 32 rows name the same one
Outputs:
- learnability: float32 [16384], P(('dp', 'tower'))
- head_grad: float32 [1152, 1152], P('tower')
- owner_loss: float32 [32], P('dp')
Inputs may be any that keep to these rules, and one draw needn't show every extreme that they name: `kept_index`: the 256 entries of one index of dp are distinct. `kept_owner`: among the 256 rows of one index of dp, no owner is named more than 32 times, a bound that some block reaches.
All inputs are finite; a program needn't handle non-finite values.
Results may differ from a plain program's by a relative error of at most 0.0029.
Values may be sent and summed in bfloat16 or wider, within the bound.
A program may use at most 32 MiB of HBM per device.

v0:
```python
import math

import jax
import jax.numpy as jnp
from jax import lax
from jax.sharding import PartitionSpec as P


def pair_terms(image, text_piece, positive, logit_scale, pair_count):
    logits = (
        lax.dot_general(
            image, text_piece, (((1,), (1,)), ((), ())), preferred_element_type=jnp.float32
        )
        * logit_scale
    )
    values = jnp.where(positive, jax.nn.softplus(-logits), jax.nn.softplus(logits) / pair_count)
    return jnp.sum(values, 1)


def local(learner_image, learner_text, ref_image, ref_text, head_weight, kept_index, kept_owner):
    pair_count = learner_image.shape[0]
    model_width = head_weight.shape[1]
    column_width = head_weight.shape[0]
    logit_scale = 1.0 / math.sqrt(model_width)
    dp_index = lax.axis_index("dp")
    tower_index = lax.axis_index("tower")
    tower_count = lax.axis_size("tower")
    dp_count = lax.axis_size("dp")
    rows_each = pair_count // tower_count
    own_rows = dp_index * pair_count + jnp.arange(pair_count, dtype=jnp.int32)
    kept_image = learner_image[kept_index]
    kept_text = learner_text[kept_index]
    text_cols = lax.dynamic_slice_in_dim(
        kept_text, tower_index * column_width, column_width, 1
    ).astype(jnp.float32)
    projected = lax.dot_general(
        kept_image, head_weight, (((1,), (1,)), ((), ())), preferred_element_type=jnp.float32
    )
    logit_part = jnp.sum(projected * text_cols, 1)
    text_l = lax.dynamic_slice_in_dim(learner_text, tower_index * rows_each, rows_each, 0)
    text_r = lax.dynamic_slice_in_dim(ref_text, tower_index * rows_each, rows_each, 0)
    pieces = (
        lax.all_gather(text_l, "dp", axis=0, tiled=True),
        lax.all_gather(text_r, "dp", axis=0, tiled=True),
    )
    gathered_row = jnp.arange(pieces[0].shape[0], dtype=jnp.int32)
    column_ids = (
        gathered_row // rows_each * pair_count + tower_index * rows_each + gathered_row % rows_each
    )
    positive = own_rows[:, None] == column_ids[None, :]
    totals_l = pair_terms(learner_image, pieces[0], positive, logit_scale, pair_count)
    totals_r = pair_terms(ref_image, pieces[1], positive, logit_scale, pair_count)
    diff_all, logit_total = lax.psum((totals_l - totals_r, logit_part), "tower")
    learnability = lax.dynamic_slice_in_dim(diff_all, tower_index * rows_each, rows_each)
    head_logit = logit_total * logit_scale
    head_loss = jax.nn.softplus(-head_logit)
    head_slope = -jax.nn.sigmoid(-head_logit) * logit_scale
    slope_text = (head_slope[:, None] * text_cols).astype(jnp.bfloat16)
    grad_part = lax.dot_general(
        slope_text, kept_image, (((0,), (0,)), ((), ())), preferred_element_type=jnp.float32
    )
    targets = jnp.arange(dp_count, dtype=jnp.int32)
    owner_table = (kept_owner[:, 0][:, None] == targets[None, :]).astype(jnp.float32)
    loss_vector = jnp.sum(owner_table * head_loss[:, None], 0)
    head_grad, loss_all = lax.psum((grad_part, loss_vector), "dp")
    owner_loss = lax.dynamic_slice_in_dim(loss_all, dp_index, 1)
    return (learnability, head_grad, owner_loss)


def solution(mesh):
    placed = (
        P("dp", None),
        P("dp", None),
        P("dp", None),
        P("dp", None),
        P("tower", None),
        P("dp"),
        P("dp", None),
    )
    return jax.shard_map(
        local,
        mesh=mesh,
        in_specs=placed,
        out_specs=(P(("dp", "tower")), P("tower", None), P("dp")),
        check_vma=False,
    )
```

profile of v0, /device:TPU:10, one launch (start us, length us, event | category | flops | bytes accessed | tf_op | source)
XLA Modules:
  0.0 578.4 jit_solution(11836728517335789614)
XLA Ops:
  7.2 0.0 copy-start
  7.2 0.0 all-gather.3.cloned.1.call-start
  7.2 1.2 copy-done
  8.4 0.6 constant_dynamic-slice_fusion.2
  9.1 0.0 all-gather.3.cloned.1.call-update
  9.1 0.0 all-gather.5.cloned.1.call-start
  9.1 1.4 constant_dynamic-slice_fusion.1
  10.5 0.0 all-gather.5.cloned.1.call-update
  10.5 0.0 all-reduce.3.cloned.1.call-start
  10.6 0.7 compare_select_fusion.7
  11.3 0.0 copy-start.1
  11.3 1.3 gather_fusion.1
  12.6 0.1 constant_dynamic-slice_fusion
  12.7 0.1 copy.12
  12.8 0.0 copy-done.1
  12.8 0.0 copy-start.2
  12.8 1.3 gather_fusion
  14.1 0.0 copy-done.2
  14.1 0.4 fusion.2
  14.5 101.7 %all-gather.3.cloned.1.call-done = bf16[512,1152]{1,0:T(8,128)(2,1)} async-done(((bf16[16,1152]{1,0:T(8,128)(2,1)}), bf16[512,1152]{1,0:T(8,128)(2,1)}) %all-gather.3.cloned.1.call-update) | async-done | bytes 1179664 | tf_op jit(solution)/shard_map/all_gather | solution.py:43
  116.1 3.5 fusion.3
  119.6 0.0 copy-start.3
  119.7 88.7 %all-gather.5.cloned.1.call-done = bf16[512,1152]{1,0:T(8,128)(2,1)} async-done(((bf16[16,1152]{1,0:T(8,128)(2,1)}), bf16[512,1152]{1,0:T(8,128)(2,1)}) %all-gather.5.cloned.1.call-update) | async-done | bytes 1179664 | tf_op jit(solution)/shard_map/all_gather | solution.py:44
  208.4 3.9 fusion.4
  212.3 43.8 %all-reduce = (f32[512]{0:T(512)S(1)}, f32[256]{0:T(256)S(1)}) all-reduce(f32[512]{0:T(512)S(1)} %sub.10, f32[256]{0:T(256)S(1)} %fusion.2), channel_id=1, replica_groups=mesh['dp'=32,'tower'=32] {'tower'}, use_global_device_ids=true, to_apply=%region_2.3 | all-reduce | flops 768 | bytes 6144 | tf_op jit(solution)/shard_map/psum | solution.py:53
  256.1 0.9 fusion.8
  257.0 0.0 all-reduce.3.cloned.1.call-update
  257.0 0.6 dynamic_slice.17
  257.6 0.0 copy-done.3
  257.6 0.1 select_reduce_fusion
  257.7 79.7 %psum.31 = f32[32]{0:T(128)S(1)} all-reduce(f32[32]{0:T(128)S(1)} %select_reduce_fusion), channel_id=1, replica_groups=mesh['dp'=32,'tower'=32] {'dp'}, use_global_device_ids=true, to_apply=%region_7.8 | all-reduce | flops 32 | bytes 256 | tf_op jit(solution)/shard_map/psum | solution.py:65
  337.4 0.6 dynamic_slice.19
  338.0 232.3 %all-reduce.3.cloned.1.call-done = f32[36,1152]{1,0:T(8,128)} async-done(((f32[36,1152]{1,0:T(8,128)}), f32[36,1152]{1,0:T(8,128)}) %all-reduce.3.cloned.1.call-update) | async-done | bytes 165904 | tf_op jit(solution)/shard_map/psum | solution.py:65
  570.3 1.6 copy.14
  (4 shorter events, 0.0 us)
Async XLA Ops:
  7.2 1.3 copy-start
  7.2 109.0 %all-gather.3.cloned.1.call-start = ((), (), s32[]{:S(2)}) async-start(), calls=%async_computation | async-start | bytes 1216512 | tf_op jit(solution)/shard_map/all_gather | solution.py:43
  9.1 199.3 %all-gather.5.cloned.1.call-start = ((), (), s32[]{:S(2)}) async-start(), calls=%async_computation.1 | async-start | bytes 1216512 | tf_op jit(solution)/shard_map/all_gather | solution.py:44
  10.5 559.7 %all-reduce.3.cloned.1.call-start = ((), (), s32[]{:S(2)}) async-start(), calls=%async_computation.2 | async-start | bytes 368640 | tf_op jit(solution)/shard_map/psum | solution.py:65
  11.3 1.5 copy-start.1
  12.8 1.3 copy-start.2
  119.6 137.9 %copy-start.3 = (s32[256,1]{0,1:T(1,128)S(1)}, s32[256,1]{0,1:T(1,128)}, u32[]{:S(2)}) copy-start(s32[256,1]{0,1:T(1,128)} %param.13) | copy-start | bytes 3076
Sparse Core Ops, SparseCore 0:
  12.9 103.2 all-gather.2
  120.4 87.9 all-gather.4
  257.1 313.1 all-reduce.2
where the time goes:
time: 579 us; the launch traced here: 578 us
  waiting for transfers between devices  423 us (73%)
  blocking collectives  123 us (21%)
  between operations  13.8 us (2%)
  local copies, waits for them, and re-layouts  8.75 us (2%)
  matrix products  8.62 us (1%)
    psum x1, waiting for transfers between devices, local(): head_grad, loss_all = lax.psum((grad_part, loss_vector), 'dp')  232 us
    all_gather x1, waiting for transfers between devices, local(): lax.all_gather(text_l, 'dp', axis=0, tiled=True)  102 us
    all_gather x1, waiting for transfers between devices, local(): lax.all_gather(text_r, 'dp', axis=0, tiled=True)  88.7 us
    psum x1, blocking collectives, local(): head_grad, loss_all = lax.psum((grad_part, loss_vector), 'dp')  79.7 us
    psum x1, blocking collectives, local(): diff_all, logit_total = lax.psum((totals_l - totals_r, logit_part), 'tower')  43.8 us
  transfers between devices with their start and end apart: 3, of which 3 were waited for; matrix products, arithmetic and copies ran while one was open for 2% of the time, Pallas kernels for 0%

commit v1 on v0

v1 whole, which is shorter than its diff:
```python
import math

import jax
import jax.numpy as jnp
from jax import lax
from jax.experimental import pallas as pl
from jax.experimental.pallas import tpu as pltpu
from jax.sharding import PartitionSpec as P

MESH = pl.DeviceIdType.MESH
N_Y, N_ZH, N_ZL, N_X, N_C = 8, 4, 2, 8, 2
POS = (0, 2, 4, 6, 7, 5, 3, 1)
TILES = 6
LOG2E = 1.4426950408889634


def kernel(li, lt, ri, rt, w, ki, ko, learn, grad, owner,
           img, txt, wv, kiv, kov, buf, tz, tx, tsrc, lz, lx, lsrc,
           chunks, rsbuf, red, zbuf, agbuf, ls, ss, rs):
    pairs, width = img.shape[1], img.shape[2]
    cols = w.shape[0]
    piece = pairs // (N_ZL * N_X * N_C)
    block = piece * N_ZH
    scale = 1.0 / math.sqrt(width)
    d, t = lax.axis_index("dp"), lax.axis_index("tower")
    y, zh = d // N_ZH, d % N_ZH
    q, x = (t // (N_X * N_C)) * N_C + t % N_C, (t // N_C) % N_X

    def at_y(k):
        return (((y + k) % N_Y) * N_ZH + zh, t)

    def at_z(k):
        return (y * N_ZH + (zh + k) % N_ZH, t)

    def at_q(k):
        r = (q + k) % (N_ZL * N_C)
        return (d, (r // N_C) * (N_X * N_C) + x * N_C + r % N_C)

    def at_x(k):
        return (d, (q // N_C) * (N_X * N_C) + ((x + k) % N_X) * N_C + q % N_C)

    peers = [at_y(k) for k in range(1, N_Y)] + [at_z(k) for k in range(1, N_ZH)]
    peers += [at_q(k) for k in range(1, N_ZL * N_C)] + [at_x(k) for k in range(1, N_X)]
    sent = []

    def send(src, dst, device):
        i = len(sent)
        copy = pltpu.make_async_remote_copy(
            src_ref=src, dst_ref=dst, send_sem=ss.at[i], recv_sem=rs.at[i],
            device_id=device, device_id_type=MESH)
        copy.start()
        sent.append(copy)
        return copy

    barrier = pltpu.get_barrier_semaphore()
    for p in peers:
        pl.semaphore_signal(barrier, inc=1, device_id=p, device_id_type=MESH)
    own = pl.ds(pl.multiple_of(t * piece, piece), piece)
    loads = [(lt.at[own], buf.at[0, pl.ds(0, piece)]), (rt.at[own], buf.at[1, pl.ds(0, piece)]),
             (li, img.at[0]), (w, wv), (lt, txt), (ki, kiv), (ko, kov), (ri, img.at[1])]
    loads = [pltpu.make_async_copy(a, b, ls.at[i]) for i, (a, b) in enumerate(loads)]
    for c in loads:
        c.start()
    pl.semaphore_wait(barrier, len(peers))

    def rows(r, z, n):
        return pl.ds(POS[r % N_Y] * block + z * piece, n)

    z_in = {}
    y_in = {}
    texts = (lt, rt)
    for m in range(2):
        for k in (1, 3):
            z_in[m, k] = send(texts[m].at[own], buf.at[m, rows(0, N_ZH - k, piece)], at_z(k))
        for s in (1, -1):
            y_in[m, s, 0] = [send(texts[m].at[own], buf.at[m, rows(-s, 0, piece)], at_y(s))]
    for m in range(2):
        z_in[m, 2] = send(texts[m].at[own], buf.at[m, rows(0, 2, piece)], at_z(2))

    for c in loads[:5]:
        c.wait()
    nt = (((1,), (1,)), ((), ()))

    def dot_nt(a, b):
        return lax.dot_general(a, b, nt, preferred_element_type=jnp.float32)

    pad = -(-cols // 8) * 8
    col = lax.broadcasted_iota(jnp.int32, (pad, width), 0)
    place = lax.broadcasted_iota(jnp.int32, (pad, width), 1)
    choose = jnp.where((place == t * cols + col) & (col < cols), 1.0, 0.0).astype(jnp.bfloat16)
    text_cols = dot_nt(choose, txt[...])
    projected = dot_nt(wv[...], img[0])
    part = jnp.sum(projected * text_cols[:cols], 0, keepdims=True)

    def tower_sum(value, src, first, second):
        src[0] = value
        first[q] = value
        got = [send(src.at[0], first.at[q], at_q(k)) for k in range(1, N_ZL * N_C)]

        def middle():
            for c in got:
                c.wait_recv()
            value = first[0]
            for k in range(1, N_ZL * N_C):
                value = value + first[k]
            src[1] = value
            second[x] = value
            got2 = [send(src.at[1], second.at[x], at_x(k)) for k in range(1, N_X)]

            def last():
                for c in got2:
                    c.wait_recv()
                value = second[0]
                for k in range(1, N_X):
                    value = value + second[k]
                return value
            return last
        return middle

    head_middle = tower_sum(part, tsrc, tz, tx)

    for k in (1, 3, 2):
        for m in range(2):
            z_in[m, k].wait_recv()
            for s in (1, -1):
                y_in[m, s, 0].append(
                    send(buf.at[m, rows(0, N_ZH - k, piece)],
                         buf.at[m, rows(-s, N_ZH - k, piece)], at_y(s)))

    for c in loads[5:]:
        c.wait()

    lane = lax.broadcasted_iota(jnp.int32, (8, pairs), 1)
    sub = lax.broadcasted_iota(jnp.int32, (8, pairs), 0)

    def losses(m, start, count, with_own):
        logits = dot_nt(buf[m, start:start + count], img[m])
        linear = jnp.zeros((8, pairs), jnp.float32)
        prod = jnp.zeros((8, pairs), jnp.float32)
        diag = jnp.zeros((8, pairs), jnp.float32)
        for g in range(count // 8):
            v = logits[8 * g:8 * g + 8]
            e = jnp.exp2(-jnp.abs(v * (scale * LOG2E)))
            lin = jnp.maximum(v * (scale / pairs), 0.0)
            if with_own and g < piece // 8:
                is_diag = lane == t * piece + 8 * g + sub
                diag = diag + jnp.where(is_diag, jnp.maximum(-v * scale, 0.0) + jnp.log1p(e), 0.0)
                e = jnp.where(is_diag, 0.0, e)
                lin = jnp.where(is_diag, 0.0, lin)
            linear = linear + lin
            prod = prod * (1.0 + e) + e
        return diag + linear + jnp.log1p(prod) * (1.0 / pairs)

    def both(start, count, with_own=False):
        return losses(0, start, count, with_own) - losses(1, start, count, with_own)

    total = both(0, block, True)

    head_last = head_middle()

    def relay(step):
        for m in range(2):
            for s in (1, -1):
                if (m, s, step) in y_in:
                    for c in y_in[m, s, step]:
                        c.wait_recv()
                    r = -s * (step + 1)
                    if step < 2 or (step == 2 and (s == 1) == (m == 0)):
                        y_in[m, s, step + 1] = [
                            send(buf.at[m, rows(r, 0, block)], buf.at[m, rows(r - s, 0, block)], at_y(s))]

    relay(0)
    total = total + both(block, 2 * block)

    head_logit = head_last() * scale
    e = jnp.exp(-jnp.abs(head_logit))
    head_loss = jnp.maximum(-head_logit, 0.0) + jnp.log1p(e)
    slope = -(jnp.where(head_logit >= 0.0, e, 1.0) / (1.0 + e)) * scale
    kept = kiv.shape[1]
    hit = lax.broadcasted_iota(jnp.int32, (pairs, kept), 0) == kiv[...]
    hit = jnp.where(hit, 1.0, 0.0).astype(jnp.bfloat16)
    owner_plus = jnp.broadcast_to(kov[...].astype(jnp.float32) + 1.0, (16, kept)).astype(jnp.bfloat16)
    owner_of = dot_nt(owner_plus, hit)[:1]
    slope = jnp.where(owner_of > 0.5, slope, 0.0)
    slope_text = (text_cols * slope).astype(jnp.bfloat16)
    grad_part = jnp.dot(slope_text, img[0], preferred_element_type=jnp.float32)
    n_dp = N_Y * N_ZH
    each = lax.broadcasted_iota(jnp.int32, (n_dp, pairs), 0)
    mine = owner_of == (each + 1).astype(jnp.float32)
    owner_col = jnp.sum(jnp.where(mine, head_loss, 0.0), 1, keepdims=True)
    on_lane = lax.broadcasted_iota(jnp.int32, (n_dp, 128), 0) == lax.broadcasted_iota(jnp.int32, (n_dp, 128), 1)
    owner_row = jnp.sum(jnp.where(on_lane, owner_col, 0.0), 0, keepdims=True)
    wide = width // 128
    n_tiles = (pad // 8) * wide
    for i in range(N_Y * TILES):
        if i < n_tiles:
            a, b = 8 * (i // wide), 128 * (i % wide)
            tile = grad_part[a:a + 8, b:b + 128]
        elif i == n_tiles:
            tile = jnp.broadcast_to(owner_row, (8, 128))
        else:
            tile = jnp.zeros((8, 128), jnp.float32)
        chunks[i // TILES, i % TILES] = tile
    got = [send(chunks.at[(y + k) % N_Y], rsbuf.at[k - 1], at_y(k)) for k in range(1, N_Y)]

    relay(1)
    total = total + both(3 * block, 2 * block)

    for c in got:
        c.wait_recv()
    value = chunks[y]
    for k in range(N_Y - 1):
        value = value + rsbuf[k]
    red[...] = value
    zbuf[zh] = value
    got = [send(red, zbuf.at[zh], at_z(k)) for k in range(1, N_ZH)]

    relay(2)
    total = total + both(5 * block, 2 * block)

    for c in got:
        c.wait_recv()
    value = zbuf[0]
    for k in range(1, N_ZH):
        value = value + zbuf[k]
    agbuf[y] = value
    got = [send(agbuf.at[y], agbuf.at[y], at_y(k)) for k in range(1, N_Y)]

    relay(3)
    total = total + both(7 * block, block)
    learn_middle = tower_sum(jnp.sum(total, 0, keepdims=True), lsrc, lz, lx)

    for c in got:
        c.wait_recv()
    for i in range(n_tiles):
        a, b = 8 * (i // wide), 128 * (i % wide)
        n = min(8, cols - a)
        grad[a:a + n, b:b + 128] = agbuf[i // TILES, i % TILES][:n]
    all_owners = agbuf[n_tiles // TILES, n_tiles % TILES][:1]
    pick = lax.broadcasted_iota(jnp.int32, (1, 128), 1) == d
    owner[...] = jnp.broadcast_to(jnp.sum(jnp.where(pick, all_owners, 0.0), 1, keepdims=True), (1, 128))

    learn_last = learn_middle()
    diff = learn_last()
    moved = pltpu.roll(jnp.broadcast_to(diff, (8, pairs)), (pairs - t * piece) % pairs, 1)
    learn[...] = moved[:1, :128]
    for c in sent:
        c.wait_send()


def local(learner_image, learner_text, ref_image, ref_text, head_weight, kept_index, kept_owner):
    pairs, width = learner_image.shape
    cols = head_weight.shape[0]
    kept = kept_index.shape[0]
    f32, bf16, i32 = jnp.float32, jnp.bfloat16, jnp.int32
    any_space = pl.BlockSpec(memory_space=pl.ANY)
    vmem = pl.BlockSpec(memory_space=pltpu.VMEM)
    learn, grad, owner = pl.pallas_call(
        kernel,
        out_shape=(
            jax.ShapeDtypeStruct((1, 128), f32),
            jax.ShapeDtypeStruct((cols, width), f32),
            jax.ShapeDtypeStruct((1, 128), f32),
        ),
        in_specs=[any_space] * 7,
        out_specs=(vmem, vmem, vmem),
        scratch_shapes=[
            pltpu.VMEM((2, pairs, width), bf16),
            pltpu.VMEM((pairs, width), bf16),
            pltpu.VMEM((cols, width), bf16),
            pltpu.VMEM((1, kept), i32),
            pltpu.VMEM((1, kept), i32),
            pltpu.VMEM((2, pairs, width), bf16),
            pltpu.VMEM((4, 1, pairs), f32),
            pltpu.VMEM((8, 1, pairs), f32),
            pltpu.VMEM((2, 1, pairs), f32),
            pltpu.VMEM((4, 1, pairs), f32),
            pltpu.VMEM((8, 1, pairs), f32),
            pltpu.VMEM((2, 1, pairs), f32),
            pltpu.VMEM((N_Y, TILES, 8, 128), f32),
            pltpu.VMEM((N_Y - 1, TILES, 8, 128), f32),
            pltpu.VMEM((TILES, 8, 128), f32),
            pltpu.VMEM((N_ZH, TILES, 8, 128), f32),
            pltpu.VMEM((N_Y, TILES, 8, 128), f32),
            pltpu.SemaphoreType.DMA((8,)),
            pltpu.SemaphoreType.DMA((96,)),
            pltpu.SemaphoreType.DMA((96,)),
        ],
        compiler_params=pltpu.CompilerParams(
            collective_id=0, has_side_effects=True, vmem_limit_bytes=40 * 1024 * 1024
        ),
    )(
        learner_image,
        learner_text,
        ref_image,
        ref_text,
        head_weight,
        kept_index.reshape(1, kept),
        kept_owner.reshape(1, kept),
    )
    return learn[0, : pairs // 32], grad, owner[0, :1]


def solution(mesh):
    placed = (
        P("dp", None),
        P("dp", None),
        P("dp", None),
        P("dp", None),
        P("tower", None),
        P("dp"),
        P("dp", None),
    )
    return jax.shard_map(
        local,
        mesh=mesh,
        in_specs=placed,
        out_specs=(P(("dp", "tower")), P("tower", None), P("dp")),
        check_vma=False,
    )
```

time: 579 us -> 80.4 us (0.14)
  the two profiles are of different devices: /device:TPU:10 before, /device:TPU:1 now
where the time goes in v1:
time: 80.4 us; the launch traced here: 80 us
  Pallas kernels  69.7 us (87%)
  local copies, waits for them, and re-layouts  8.51 us (11%)
  between operations  1.82 us (2%)
    pallas_call x1, Pallas kernels, local(): pl.pallas_call(kernel, out_shape=(jax.ShapeDtypeStruct((1, 128), f32), ja...  69.7 us
    unnamed x15, local copies, waits for them, and re-layouts  7.99 us

profile of v1, /device:TPU:1, one launch (start us, length us, event | category | flops | bytes accessed | tf_op | source)
XLA Modules:
  0.0 80.0 jit_solution(18142125335730621013)
XLA Ops:
  0.6 0.0 copy-start
  0.6 1.3 %copy-done = bf16[512,1152]{1,0:T(8,128)(2,1)S(1)} copy-done((bf16[512,1152]{1,0:T(8,128)(2,1)S(1)}, bf16[512,1152]{1,0:T(8,128)(2,1)}, u32[]{:S(2)}) %copy-start) | copy-done | bytes 1179672
  1.9 0.0 copy-start.1
  1.9 1.3 %copy-done.1 = bf16[512,1152]{1,0:T(8,128)(2,1)S(1)} copy-done((bf16[512,1152]{1,0:T(8,128)(2,1)S(1)}, bf16[512,1152]{1,0:T(8,128)(2,1)}, u32[]{:S(2)}) %copy-start.1) | copy-done | bytes 1179672
  3.2 0.0 copy-start.2
  3.2 1.3 %copy-done.2 = bf16[512,1152]{1,0:T(8,128)(2,1)S(1)} copy-done((bf16[512,1152]{1,0:T(8,128)(2,1)S(1)}, bf16[512,1152]{1,0:T(8,128)(2,1)}, u32[]{:S(2)}) %copy-start.2) | copy-done | bytes 1179672
  4.4 0.0 copy-start.3
  4.4 1.3 %copy-done.3 = bf16[512,1152]{1,0:T(8,128)(2,1)S(1)} copy-done((bf16[512,1152]{1,0:T(8,128)(2,1)S(1)}, bf16[512,1152]{1,0:T(8,128)(2,1)}, u32[]{:S(2)}) %copy-start.3) | copy-done | bytes 1179672
  5.7 0.0 copy-start.4
  5.7 0.9 %copy-done.4 = bf16[36,1152]{1,0:T(8,128)(2,1)S(1)} copy-done((bf16[36,1152]{1,0:T(8,128)(2,1)S(1)}, bf16[36,1152]{1,0:T(8,128)(2,1)}, u32[]{:S(2)}) %copy-start.4) | copy-done | bytes 82968
  6.6 0.0 copy-start.5
  6.6 0.7 copy-done.5
  7.3 0.0 copy-start.6
  7.3 0.7 copy-done.6
  8.0 69.7 %shard_map.94 = (f32[1,128]{1,0:T(1,128)S(1)}, f32[36,1152]{1,0:T(8,128)S(1)}, f32[1,128]{1,0:T(1,128)S(1)}) custom-call(bf16[512,1152]{1,0:T(8,128)(2,1)S(1)} %copy-done, bf16[512,1152]{1,0:T(8,128)(2,1)S(1)} %copy-done.1, bf16[512,1152]{1,0:T(8,128)(2,1)S(1)} %copy-done.2, bf16[512,1152]{1,0:T(8,128)(2,1)S(1)} %copy-done.3, ...), custom_call_target="tpu_custom_call" | custom-call | tf_op jit(solution)/shard_map/pallas_call | solution.py:258
  77.7 0.5 slice_bitcast_fusion
  78.2 0.7 copy.12
Async XLA Ops:
  0.6 1.3 %copy-start = (bf16[512,1152]{1,0:T(8,128)(2,1)S(1)}, bf16[512,1152]{1,0:T(8,128)(2,1)}, u32[]{:S(2)}) copy-start(bf16[512,1152]{1,0:T(8,128)(2,1)} %li.1) | copy-start | bytes 3538948
  1.9 1.3 %copy-start.1 = (bf16[512,1152]{1,0:T(8,128)(2,1)S(1)}, bf16[512,1152]{1,0:T(8,128)(2,1)}, u32[]{:S(2)}) copy-start(bf16[512,1152]{1,0:T(8,128)(2,1)} %lt.1) | copy-start | bytes 3538948
  3.2 1.3 %copy-start.2 = (bf16[512,1152]{1,0:T(8,128)(2,1)S(1)}, bf16[512,1152]{1,0:T(8,128)(2,1)}, u32[]{:S(2)}) copy-start(bf16[512,1152]{1,0:T(8,128)(2,1)} %ri.1) | copy-start | bytes 3538948
  4.4 1.3 %copy-start.3 = (bf16[512,1152]{1,0:T(8,128)(2,1)S(1)}, bf16[512,1152]{1,0:T(8,128)(2,1)}, u32[]{:S(2)}) copy-start(bf16[512,1152]{1,0:T(8,128)(2,1)} %rt.1) | copy-start | bytes 3538948
  5.7 0.9 %copy-start.4 = (bf16[36,1152]{1,0:T(8,128)(2,1)S(1)}, bf16[36,1152]{1,0:T(8,128)(2,1)}, u32[]{:S(2)}) copy-start(bf16[36,1152]{1,0:T(8,128)(2,1)} %w.1) | copy-start | bytes 248836
  6.6 0.7 copy-start.5
  7.3 0.7 copy-start.6

commit v2 on v1

v2 whole, which is shorter than its diff:
```python
import math

import jax
import jax.numpy as jnp
from jax import lax
from jax.experimental import pallas as pl
from jax.experimental.pallas import tpu as pltpu
from jax.sharding import PartitionSpec as P

MESH = pl.DeviceIdType.MESH
N_Y, N_ZH, N_ZL, N_X, N_C = 8, 4, 2, 8, 2
POS = (0, 2, 4, 6, 7, 5, 3, 1)
ZPOS = (0, 1, 3, 2)
TILES = 6
LOG2E = 1.4426950408889634


def wrap(v, n):
    return jnp.where(v >= n, v - n, v)


def kernel(li, lt, ri, rt, w, ki, ko, learn, grad, owner,
           img, txt, wv, kiv, kov, buf, hsrc, hall, lsrc, lall,
           chunks, rsbuf, red, zbuf, agbuf, ls, ss, rs, many):
    pairs, width = img.shape[1], img.shape[2]
    cols = w.shape[0]
    n_tower = N_ZL * N_X * N_C
    piece = pairs // n_tower
    split = 6 * width // 9
    scale = 1.0 / math.sqrt(width)
    d, t = lax.axis_index("dp"), lax.axis_index("tower")
    y = d // N_ZH
    zh = d - y * N_ZH
    zl = t // (N_X * N_C)
    xc = t - zl * (N_X * N_C)
    x = xc // N_C
    c = xc - x * N_C
    ys = [wrap(y + k, N_Y) for k in range(N_Y)]
    at_y = [(ys[k] * N_ZH + zh, t) for k in range(N_Y)]
    at_z = [(y * N_ZH + wrap(zh + k, N_ZH), t) for k in range(N_ZH)]
    at_t = []
    for k in (4, 3, 5, 2, 6, 1, 7, 0):
        xk = wrap(x + k, N_X)
        for dz in (1, 0):
            zk = 1 - zl if dz else zl
            for dc in (1, 0):
                if k or dz or dc:
                    tk = zk * (N_X * N_C) + xk * N_C + (1 - c if dc else c)
                    at_t.append(((d, tk), zk * 2 + jnp.where(xk >= N_X // 2, 1, 0)))

    peers = at_y[1:] + at_z[1:] + [p for p, _ in at_t]
    sent = []

    def send(src, dst, device):
        i = len(sent)
        copy = pltpu.make_async_remote_copy(
            src_ref=src, dst_ref=dst, send_sem=ss.at[i], recv_sem=rs.at[i],
            device_id=device, device_id_type=MESH)
        copy.start()
        sent.append(copy)
        return copy

    def to_tower(src_of, dst, sems):
        for p, tile in at_t:
            pltpu.make_async_remote_copy(
                src_ref=src_of(tile), dst_ref=dst, send_sem=many.at[sems], recv_sem=many.at[sems + 1],
                device_id=p, device_id_type=MESH).start()

    def wait_tower(ref, sem):
        other = ref.at[pl.ds(0, n_tower - 1)]
        pltpu.make_async_copy(other, other, many.at[sem]).wait()

    barrier = pltpu.get_barrier_semaphore()
    for p in peers:
        pl.semaphore_signal(barrier, inc=1, device_id=p, device_id_type=MESH)
    own = pl.ds(pl.multiple_of(t * piece, piece), piece)
    loads = [(lt.at[own], buf.at[0, 0, 0]), (rt.at[own], buf.at[1, 0, 0]),
             (li, img.at[0]), (w, wv), (lt, txt), (ki, kiv), (ko, kov), (ri, img.at[1])]
    loads = [pltpu.make_async_copy(a, b, ls.at[i]) for i, (a, b) in enumerate(loads)]
    for copy in loads:
        copy.start()
    pl.semaphore_wait(barrier, len(peers))

    low, high = pl.ds(0, split), pl.ds(split, width - split)
    full = pl.ds(0, width)
    texts = (lt, rt)
    z_in = {}
    for m in range(2):
        for k in (1, 3):
            z_in[m, k] = send(texts[m].at[own, low], buf.at[m, 0, ZPOS[N_ZH - k], :, low], at_z[k])

    class Ring:
        def __init__(self, places, lanes):
            self.places, self.lanes, self.copies = places, lanes, {}

        def at(self, m, r):
            return buf.at[m, POS[r % N_Y], self.places, :, self.lanes]

        def step(self, n, m, s, src=None):
            r = -s * n
            self.copies[n, m, s] = send(self.at(m, r) if src is None else src, self.at(m, r - s), at_y[s % N_Y])

        def start(self):
            for m in range(2):
                for s in (1, -1):
                    self.step(0, m, s)

        def relay(self, n):
            for m in range(2):
                for s in (1, -1):
                    if (n, m, s) in self.copies:
                        self.copies[n, m, s].wait_recv()
                        if n < 2 or (n == 2 and (s == 1) == (m == 0)):
                            self.step(n + 1, m, s)

    ring0 = Ring(0, full)
    ring1 = Ring(pl.ds(1, 2), low)
    ring2 = Ring(3, low)
    for m in range(2):
        for s in (1, -1):
            ring0.step(0, m, s, texts[m].at[own])

    def z_relay(copies, a, n, lanes):
        for m in range(2):
            for k in (1, 3):
                copies[m, k].wait_recv()
        for m, k in ((0, 1), (1, 3)):
            copies[m, 2] = send(buf.at[m, pl.ds(a, n), ZPOS[N_ZH - k], :, lanes],
                                buf.at[m, pl.ds(a, n), 3, :, lanes], at_z[k])

    def z_high(a, n):
        copies = {}
        for m in range(2):
            for k in (1, 3):
                copies[m, k] = send(buf.at[m, pl.ds(a, n), 0, :, high],
                                    buf.at[m, pl.ds(a, n), ZPOS[N_ZH - k], :, high], at_z[k])
        return copies

    for copy in loads[:5]:
        copy.wait()
    nt = (((1,), (1,)), ((), ()))

    def dot_nt(a, b):
        return lax.dot_general(a, b, nt, preferred_element_type=jnp.float32)

    pad = -(-cols // 8) * 8
    col = lax.broadcasted_iota(jnp.int32, (pad, width), 0)
    place = lax.broadcasted_iota(jnp.int32, (pad, width), 1)
    choose = jnp.where((place == t * cols + col) & (col < cols), 1.0, 0.0).astype(jnp.bfloat16)
    text_cols = dot_nt(choose, txt[...])
    projected = dot_nt(wv[...], img[0])
    part = jnp.sum(projected * text_cols[:cols], 0, keepdims=True)
    hsrc[...] = part
    hall[t] = part
    to_tower(lambda tile: hsrc, hall.at[t], 0)

    ring0.relay(0)
    high_a = z_high(0, 3)
    z_relay(z_in, 0, 1, low)
    ring1.start()
    ring0.relay(1)
    for m in range(2):
        z_in[m, 2].wait_recv()
    ring2.start()
    ring1.relay(0)
    ring0.relay(2)
    for copy in loads[5:]:
        copy.wait()
    z_relay(high_a, 0, 3, high)
    ring2.relay(0)
    ring1.relay(1)
    ring0.relay(3)
    high_b = z_high(3, N_Y - 3)

    lane = lax.broadcasted_iota(jnp.int32, (8, pairs), 1)
    sub = lax.broadcasted_iota(jnp.int32, (8, pairs), 0)

    def losses(m, start, count, with_own):
        text = buf[m, :, start:start + count].reshape(N_Y * count * piece, width)
        logits = dot_nt(text, img[m])
        linear = jnp.zeros((8, pairs), jnp.float32)
        prod = jnp.zeros((8, pairs), jnp.float32)
        logs = jnp.zeros((8, pairs), jnp.float32)
        diag = jnp.zeros((8, pairs), jnp.float32)
        groups = text.shape[0] // 8
        for g in range(groups):
            v = logits[8 * g:8 * g + 8]
            e = jnp.exp2(-jnp.abs(v * (scale * LOG2E)))
            lin = jnp.maximum(v * (scale / pairs), 0.0)
            if with_own and g < piece // 8:
                is_diag = lane == t * piece + 8 * g + sub
                diag = diag + jnp.where(is_diag, jnp.maximum(-v * scale, 0.0) + jnp.log1p(e), 0.0)
                e = jnp.where(is_diag, 0.0, e)
                lin = jnp.where(is_diag, 0.0, lin)
            linear = linear + lin
            prod = prod * (1.0 + e) + e
            if g % 16 == 15 or g == groups - 1:
                logs = logs + jnp.log1p(prod)
                prod = jnp.zeros((8, pairs), jnp.float32)
        return diag + linear + logs * (1.0 / pairs)

    def both(start, count, with_own=False):
        return losses(0, start, count, with_own) - losses(1, start, count, with_own)

    total = both(0, 1, True)

    wait_tower(hall, 1)
    head_logit = jnp.sum(hall[...], 0) * scale
    e = jnp.exp(-jnp.abs(head_logit))
    head_loss = jnp.maximum(-head_logit, 0.0) + jnp.log1p(e)
    slope = -(jnp.where(head_logit >= 0.0, e, 1.0) / (1.0 + e)) * scale
    kept = kiv.shape[1]
    hit = lax.broadcasted_iota(jnp.int32, (pairs, kept), 0) == kiv[...]
    hit = jnp.where(hit, 1.0, 0.0).astype(jnp.bfloat16)
    owner_plus = jnp.broadcast_to(kov[...].astype(jnp.float32) + 1.0, (16, kept)).astype(jnp.bfloat16)
    owner_of = dot_nt(owner_plus, hit)[:1]
    slope = jnp.where(owner_of > 0.5, slope, 0.0)
    slope_text = (text_cols * slope).astype(jnp.bfloat16)
    grad_part = jnp.dot(slope_text, img[0], preferred_element_type=jnp.float32)
    n_dp = N_Y * N_ZH
    each = lax.broadcasted_iota(jnp.int32, (n_dp, pairs), 0)
    mine = owner_of == (each + 1).astype(jnp.float32)
    owner_col = jnp.sum(jnp.where(mine, head_loss, 0.0), 1, keepdims=True)
    on_lane = lax.broadcasted_iota(jnp.int32, (n_dp, 128), 0) == lax.broadcasted_iota(jnp.int32, (n_dp, 128), 1)
    owner_row = jnp.sum(jnp.where(on_lane, owner_col, 0.0), 0, keepdims=True)
    wide = width // 128
    n_tiles = (pad // 8) * wide
    for i in range(N_Y * TILES):
        if i < n_tiles:
            a, b = 8 * (i // wide), 128 * (i % wide)
            tile = grad_part[a:a + 8, b:b + 128]
        elif i == n_tiles:
            tile = jnp.broadcast_to(owner_row, (8, 128))
        else:
            tile = jnp.zeros((8, 128), jnp.float32)
        chunks[i // TILES, i % TILES] = tile
    scattered = [send(chunks.at[ys[k]], rsbuf.at[k - 1], at_y[k]) for k in (4, 3, 5, 2, 6, 1, 7)]

    ring2.relay(1)
    ring1.relay(2)
    for m in range(2):
        high_a[m, 2].wait_recv()
    ring2.relay(2)
    z_relay(high_b, 3, N_Y - 3, high)

    for copy in scattered:
        copy.wait_recv()
    value = chunks[y]
    for k in range(N_Y - 1):
        value = value + rsbuf[k]
    red[...] = value
    zbuf[zh] = value
    summed = [send(red, zbuf.at[zh], at_z[k]) for k in (2, 1, 3)]

    ring1.relay(3)
    total = total + both(1, 2)

    for copy in summed:
        copy.wait_recv()
    value = zbuf[0]
    for k in range(1, N_ZH):
        value = value + zbuf[k]
    rest = value - value.astype(jnp.bfloat16).astype(jnp.float32)
    at = lax.broadcasted_iota(jnp.int32, value.shape, 0) * 8 + lax.broadcasted_iota(jnp.int32, value.shape, 1)
    low_half = (at >= 8 * (n_tiles % TILES) + 4) & (at < 8 * (n_tiles % TILES) + 8) & (y == n_tiles // TILES)
    value = jnp.where(low_half, rest, value)
    agbuf[y] = value.reshape(8 * TILES, 128).astype(jnp.bfloat16)
    gathered = [send(agbuf.at[y], agbuf.at[y], at_y[k]) for k in (4, 3, 5, 2, 6, 1, 7)]

    ring2.relay(3)
    for m in range(2):
        high_b[m, 2].wait_recv()
    total = total + both(3, 1)

    diff = jnp.sum(total, 0, keepdims=True)
    for i in range(pairs // 128):
        lsrc[i] = diff[:, 128 * i:128 * i + 128]
    own_tile = zl * 2 + jnp.where(x >= N_X // 2, 1, 0)
    lall[t] = lsrc[own_tile]
    to_tower(lambda tile: lsrc.at[tile], lall.at[t], 2)

    for copy in gathered:
        copy.wait_recv()
    for i in range(n_tiles):
        a, b = 8 * (i // wide), 128 * (i % wide)
        n, r = min(8, cols - a), 8 * (i % TILES)
        if i % 2 == 0:
            pair = agbuf[i // TILES, r:r + 16].astype(jnp.float32)
        grad[a:a + n, b:b + 128] = pair[8 * (i % 2):8 * (i % 2) + n]
    r = 8 * (n_tiles % TILES) // 16 * 16
    pair = agbuf[n_tiles // TILES, r:r + 16].astype(jnp.float32)
    pair = pair[8 * (n_tiles % 2):8 * (n_tiles % 2) + 8]
    all_owners = pair[:1] + pair[4:5]
    pick = lax.broadcasted_iota(jnp.int32, (1, 128), 1) == d
    owner[...] = jnp.broadcast_to(jnp.sum(jnp.where(pick, all_owners, 0.0), 1, keepdims=True), (1, 128))

    wait_tower(lall, 3)
    rows = jnp.broadcast_to(jnp.sum(lall[...], 0), (8, 128))
    first = (xc - jnp.where(x >= N_X // 2, N_X, 0)) * piece
    learn[...] = pltpu.roll(rows, jnp.where(first > 0, 128 - first, 0), 1)[:1]
    wait_tower(hall, 0)
    wait_tower(lall, 2)
    for copy in sent:
        copy.wait_send()


def local(learner_image, learner_text, ref_image, ref_text, head_weight, kept_index, kept_owner):
    pairs, width = learner_image.shape
    cols = head_weight.shape[0]
    kept = kept_index.shape[0]
    f32, bf16, i32 = jnp.float32, jnp.bfloat16, jnp.int32
    any_space = pl.BlockSpec(memory_space=pl.ANY)
    vmem = pl.BlockSpec(memory_space=pltpu.VMEM)
    learn, grad, owner = pl.pallas_call(
        kernel,
        out_shape=(
            jax.ShapeDtypeStruct((1, 128), f32),
            jax.ShapeDtypeStruct((cols, width), f32),
            jax.ShapeDtypeStruct((1, 128), f32),
        ),
        in_specs=[any_space] * 7,
        out_specs=(vmem, vmem, vmem),
        scratch_shapes=[
            pltpu.VMEM((2, pairs, width), bf16),
            pltpu.VMEM((pairs, width), bf16),
            pltpu.VMEM((cols, width), bf16),
            pltpu.VMEM((1, kept), i32),
            pltpu.VMEM((1, kept), i32),
            pltpu.VMEM((2, N_Y, N_ZH, pairs // 32, width), bf16),
            pltpu.VMEM((1, pairs), f32),
            pltpu.VMEM((32, 1, pairs), f32),
            pltpu.VMEM((4, 1, 128), f32),
            pltpu.VMEM((32, 1, 128), f32),
            pltpu.VMEM((N_Y, TILES, 8, 128), f32),
            pltpu.VMEM((N_Y - 1, TILES, 8, 128), f32),
            pltpu.VMEM((TILES, 8, 128), f32),
            pltpu.VMEM((N_ZH, TILES, 8, 128), f32),
            pltpu.VMEM((N_Y, 8 * TILES, 128), bf16),
            pltpu.SemaphoreType.DMA((8,)),
            pltpu.SemaphoreType.DMA((96,)),
            pltpu.SemaphoreType.DMA((96,)),
            pltpu.SemaphoreType.DMA((4,)),
        ],
        compiler_params=pltpu.CompilerParams(
            collective_id=0, has_side_effects=True, vmem_limit_bytes=62 * 1024 * 1024
        ),
    )(
        learner_image,
        learner_text,
        ref_image,
        ref_text,
        head_weight,
        kept_index.reshape(1, kept),
        kept_owner.reshape(1, kept),
    )
    return learn[0, : pairs // 32], grad, owner[0, :1]


def solution(mesh):
    placed = (
        P("dp", None),
        P("dp", None),
        P("dp", None),
        P("dp", None),
        P("tower", None),
        P("dp"),
        P("dp", None),
    )
    return jax.shard_map(
        local,
        mesh=mesh,
        in_specs=placed,
        out_specs=(P(("dp", "tower")), P("tower", None), P("dp")),
        check_vma=False,
    )
```

time: 80.4 us -> 68.6 us (0.85)
  Pallas kernels: 69.7 us -> 63.3 us
  local copies, waits for them, and re-layouts: 8.51 us -> 2.74 us
    pallas_call x1, Pallas kernels: 69.7 us -> 63.3 us  [local(): pl.pallas_call(kernel, out_shape=(jax.ShapeDtypeStruct((1, 128), f32), ja...]
    unnamed x15 -> x1, local copies, waits for them, and re-layouts: 7.99 us -> 1.61 us
where the time goes in v2:
time: 68.6 us; the launch traced here: 68.4 us
  Pallas kernels  63.3 us (92%)
  local copies, waits for them, and re-layouts  2.74 us (4%)
  between operations  2.33 us (3%)
    pallas_call x1, Pallas kernels, local(): pl.pallas_call(kernel, out_shape=(jax.ShapeDtypeStruct((1, 128), f32), ja...  63.3 us
    unnamed x1, local copies, waits for them, and re-layouts  1.61 us

profile of v2, /device:TPU:1, one launch (start us, length us, event | category | flops | bytes accessed | tf_op | source)
XLA Modules:
  0.0 68.4 jit_solution(13173807173502553454)
XLA Ops:
  0.6 63.3 %shard_map.94 = (f32[1,128]{1,0:T(1,128)}, f32[36,1152]{1,0:T(8,128)}, f32[1,128]{1,0:T(1,128)}) custom-call(bf16[512,1152]{1,0:T(8,128)(2,1)} %li.1, bf16[512,1152]{1,0:T(8,128)(2,1)} %lt.1, bf16[512,1152]{1,0:T(8,128)(2,1)} %ri.1, bf16[512,1152]{1,0:T(8,128)(2,1)} %rt.1, bf16[36,1152]{1,0:T(8,128)(2,1)} %w.1, s32[1,256]{1,0:T(1,128)} %bitcast.6, ...), custom_call_target="tpu_custom_call" | custom-call | tf_op jit(solution)/shard_map/pallas_call | solution.py:314
  63.9 1.1 %slice_bitcast_fusion = f32[16]{0:T(128)} fusion(f32[1,128]{1,0:T(1,128)} %get-tuple-element.6), kind=kLoop, calls=%fused_computation | loop fusion | bytes 128 | tf_op jit(solution)/shard_map/squeeze | solution.py:356
  65.1 1.6 %copy.12 = f32[36,1152]{1,0:T(8,128)} copy(f32[36,1152]{1,0:T(8,128)} %get-tuple-element.13) | data formatting | bytes 331776

commit v3 on v2

--- a/solution.py
+++ b/solution.py
@@ -70,24 +70,24 @@
         other = ref.at[pl.ds(0, n_tower - 1)]
         pltpu.make_async_copy(other, other, many.at[sem]).wait()
 
-    barrier = pltpu.get_barrier_semaphore()
-    for p in peers:
-        pl.semaphore_signal(barrier, inc=1, device_id=p, device_id_type=MESH)
     own = pl.ds(pl.multiple_of(t * piece, piece), piece)
     loads = [(lt.at[own], buf.at[0, 0, 0]), (rt.at[own], buf.at[1, 0, 0]),
              (li, img.at[0]), (w, wv), (lt, txt), (ki, kiv), (ko, kov), (ri, img.at[1])]
     loads = [pltpu.make_async_copy(a, b, ls.at[i]) for i, (a, b) in enumerate(loads)]
     for copy in loads:
         copy.start()
+    barrier = pltpu.get_barrier_semaphore()
+    for p in peers:
+        pl.semaphore_signal(barrier, inc=1, device_id=p, device_id_type=MESH)
+    loads[0].wait()
+    loads[1].wait()
     pl.semaphore_wait(barrier, len(peers))
 
     low, high = pl.ds(0, split), pl.ds(split, width - split)
     full = pl.ds(0, width)
-    texts = (lt, rt)
     z_in = {}
-    for m in range(2):
-        for k in (1, 3):
-            z_in[m, k] = send(texts[m].at[own, low], buf.at[m, 0, ZPOS[N_ZH - k], :, low], at_z[k])
+    for k in (1, 3):
+        z_in[k] = send(buf.at[:, 0, 0, :, low], buf.at[:, 0, ZPOS[N_ZH - k], :, low], at_z[k])
 
     class Ring:
         def __init__(self, places, lanes):
@@ -96,47 +96,41 @@
         def at(self, m, r):
             return buf.at[m, POS[r % N_Y], self.places, :, self.lanes]
 
-        def step(self, n, m, s, src=None):
+        def step(self, n, s):
             r = -s * n
-            self.copies[n, m, s] = send(self.at(m, r) if src is None else src, self.at(m, r - s), at_y[s % N_Y])
+            m = slice(None) if n < 3 else (0 if s == 1 else 1)
+            self.copies[n, s] = send(self.at(m, r), self.at(m, r - s), at_y[s % N_Y])
 
         def start(self):
-            for m in range(2):
-                for s in (1, -1):
-                    self.step(0, m, s)
+            for s in (1, -1):
+                self.step(0, s)
 
         def relay(self, n):
-            for m in range(2):
-                for s in (1, -1):
-                    if (n, m, s) in self.copies:
-                        self.copies[n, m, s].wait_recv()
-                        if n < 2 or (n == 2 and (s == 1) == (m == 0)):
-                            self.step(n + 1, m, s)
+            for s in (1, -1):
+                self.copies[n, s].wait_recv()
+                if n < 3:
+                    self.step(n + 1, s)
 
     ring0 = Ring(0, full)
     ring1 = Ring(pl.ds(1, 2), low)
     ring2 = Ring(3, low)
-    for m in range(2):
-        for s in (1, -1):
-            ring0.step(0, m, s, texts[m].at[own])
+    ring0.start()
 
     def z_relay(copies, a, n, lanes):
-        for m in range(2):
-            for k in (1, 3):
-                copies[m, k].wait_recv()
+        for k in (1, 3):
+            copies[k].wait_recv()
         for m, k in ((0, 1), (1, 3)):
             copies[m, 2] = send(buf.at[m, pl.ds(a, n), ZPOS[N_ZH - k], :, lanes],
                                 buf.at[m, pl.ds(a, n), 3, :, lanes], at_z[k])
 
     def z_high(a, n):
         copies = {}
-        for m in range(2):
-            for k in (1, 3):
-                copies[m, k] = send(buf.at[m, pl.ds(a, n), 0, :, high],
-                                    buf.at[m, pl.ds(a, n), ZPOS[N_ZH - k], :, high], at_z[k])
+        for k in (1, 3):
+            copies[k] = send(buf.at[:, pl.ds(a, n), 0, :, high],
+                             buf.at[:, pl.ds(a, n), ZPOS[N_ZH - k], :, high], at_z[k])
         return copies
 
-    for copy in loads[:5]:
+    for copy in loads[2:5]:
         copy.wait()
     nt = (((1,), (1,)), ((), ()))
 
@@ -238,10 +232,10 @@
 
     ring2.relay(1)
     ring1.relay(2)
+    z_relay(high_b, 3, N_Y - 3, high)
+    ring2.relay(2)
     for m in range(2):
         high_a[m, 2].wait_recv()
-    ring2.relay(2)
-    z_relay(high_b, 3, N_Y - 3, high)
 
     for copy in scattered:
         copy.wait_recv()

time: 68.6 us -> 67.5 us (0.984)
  Pallas kernels: 63.3 us -> 62.2 us
    pallas_call x1, Pallas kernels: 63.3 us -> 62.2 us  [local(): pl.pallas_call(kernel, out_shape=(jax.ShapeDtypeStruct((1, 128), f32), ja...]
where the time goes in v3:
time: 67.5 us; the launch traced here: 67.3 us
  Pallas kernels  62.2 us (92%)
  local copies, waits for them, and re-layouts  2.74 us (4%)
  between operations  2.33 us (3%)
    pallas_call x1, Pallas kernels, local(): pl.pallas_call(kernel, out_shape=(jax.ShapeDtypeStruct((1, 128), f32), ja...  62.2 us
    unnamed x1, local copies, waits for them, and re-layouts  1.61 us

profile of v3, /device:TPU:1, one launch (start us, length us, event | category | flops | bytes accessed | tf_op | source)
XLA Modules:
  0.0 67.3 jit_solution(16785114500094108848)
XLA Ops:
  0.6 62.2 %shard_map.94 = (f32[1,128]{1,0:T(1,128)}, f32[36,1152]{1,0:T(8,128)}, f32[1,128]{1,0:T(1,128)}) custom-call(bf16[512,1152]{1,0:T(8,128)(2,1)} %li.1, bf16[512,1152]{1,0:T(8,128)(2,1)} %lt.1, bf16[512,1152]{1,0:T(8,128)(2,1)} %ri.1, bf16[512,1152]{1,0:T(8,128)(2,1)} %rt.1, bf16[36,1152]{1,0:T(8,128)(2,1)} %w.1, s32[1,256]{1,0:T(1,128)} %bitcast.6, ...), custom_call_target="tpu_custom_call" | custom-call | tf_op jit(solution)/shard_map/pallas_call | solution.py:308
  62.9 1.1 %slice_bitcast_fusion = f32[16]{0:T(128)} fusion(f32[1,128]{1,0:T(1,128)} %get-tuple-element.6), kind=kLoop, calls=%fused_computation | loop fusion | bytes 128 | tf_op jit(solution)/shard_map/squeeze | solution.py:350
  64.0 1.6 %copy.12 = f32[36,1152]{1,0:T(8,128)} copy(f32[36,1152]{1,0:T(8,128)} %get-tuple-element.13) | data formatting | bytes 331776
